TPU v7x, 128 devices: a whole 4x4x4 slice. The times are simulated.
128 devices in a mesh: row: 8 (over z, core), col: 8 (over x_lo, y), depth: 2 (over x_hi).
Axes of the slice: x: 4 (x_hi: 2, x_lo: 2; x = x_hi * 2 + x_lo), y: 4, z: 4, core: 2. Of those that a mesh axis runs over, the one named last changes fastest.
Arguments:
- blocks: bfloat16 [256, 16, 4096], P('row', ('col', 'depth')), may hold values from -1 to 1
- pattern: int32 [256, 16], P('row', ('col', 'depth')), may hold values from 0 to 255, as said below
Outputs:
- purified: float32 [2048, 16384], P('row', ('col', 'depth'))
Inputs may be any that keep to these rules, and one draw needn't show every extreme that they name: `pattern`: in every block row, entries j * 1 to j + 1 - 1 name 1 different block columns of j * 16 to j * 16 + 15, in increasing order.
All inputs are finite; a program needn't handle non-finite values.
Results may differ from a plain program's by a relative error of at most 0.0028.
Values may be sent and summed in bfloat16 or wider, within the bound.
No kernel may reach another device: no remote copies, remote signals or barrier semaphores. Data moves between devices by JAX's collectives and lax.ppermute only.
A program may use at most 256 MiB of HBM per device.

v0:
```python
import jax
import jax.numpy as jnp
from jax import lax
from jax.sharding import PartitionSpec as P

BLOCK = 64
KB = 1
SR = 4


def spread(block, axis, owner):
    block = jnp.where(lax.axis_index(axis) == owner, block, jnp.zeros_like(block))
    return lax.psum(block, axis)


def densify(tiles_flat, block_ids, group_width):
    rows, slots = block_ids.shape
    groups = slots // KB
    local_ids = (block_ids % group_width).reshape(rows, groups, KB)
    onehot = (local_ids[..., None] == jnp.arange(group_width, dtype=jnp.int32)).astype(jnp.bfloat16)
    tile_grid = tiles_flat.reshape(rows, groups, KB, BLOCK, BLOCK)
    dense_tiles = jnp.einsum(
        "rgkyz,rgkc->rygcz", tile_grid, onehot, preferred_element_type=jnp.bfloat16
    )
    return dense_tiles.reshape(rows * BLOCK, groups * group_width * BLOCK)


def slab_square(slab_tiles, slab_ids, panel_dense):
    slab_rows, slots = slab_ids.shape
    width = panel_dense.shape[1]
    panel_blocks = panel_dense.reshape(-1, BLOCK, width)
    picked = panel_blocks[slab_ids]
    tile_grid = slab_tiles.reshape(slab_rows, slots, BLOCK, BLOCK)
    result = jnp.einsum("rsyz,rszc->ryc", tile_grid, picked, preferred_element_type=jnp.float32)
    return result.reshape(slab_rows * BLOCK, width)


def body(blocks, pattern):
    row_count = blocks.shape[0]
    group_width = (
        row_count * lax.axis_size("row") // (lax.axis_size("col") * lax.axis_size("depth"))
    )
    column_tiles, column_ids = (
        lax.all_gather(blocks, "row", axis=0, tiled=True),
        lax.all_gather(pattern, "row", axis=0, tiled=True),
    )
    panel_dense = densify(column_tiles, column_ids, group_width)
    row_tiles, row_ids = (
        lax.all_gather(blocks, ("col", "depth"), axis=1, tiled=True),
        lax.all_gather(pattern, ("col", "depth"), axis=1, tiled=True),
    )
    square32 = slab_square(row_tiles[:SR], row_ids[:SR], panel_dense)
    square = square32.astype(jnp.bfloat16)
    first_row = lax.axis_index(("col", "depth")) * group_width
    owner = first_row // row_count
    offset = first_row % row_count
    own_tiles = lax.dynamic_slice_in_dim(row_tiles, offset, group_width, 0)
    own_ids = lax.dynamic_slice_in_dim(row_ids, offset, group_width, 0)
    group_tiles, group_ids = (spread(own_tiles, "row", owner), spread(own_ids, "row", owner))
    group_dense = densify(group_tiles, group_ids, group_width)
    partial_value = jnp.dot(square, group_dense, preferred_element_type=jnp.float32)
    cube_sum = lax.psum_scatter(partial_value, ("col", "depth"), scatter_dimension=1, tiled=True)
    return 3.0 * square32 - 2.0 * cube_sum


def solution(mesh):
    in_specs = (P("row", ("col", "depth"), None), P("row", ("col", "depth")))
    out_specs = P("row", ("col", "depth"))
    return jax.shard_map(body, mesh=mesh, in_specs=in_specs, out_specs=out_specs, check_vma=False)
```

profile of v0, /device:TPU:1, one launch (start us, length us, event | category | flops | bytes accessed | tf_op | source)
XLA Modules:
  0.0 721.1 jit_solution(11672589581873715403)
XLA Ops:
  6.5 0.0 all-gather.4.cloned.1.call-start
  6.5 0.7 all-gather.4.cloned.1.call-update
  7.3 0.0 all-gather.6.cloned.1.call-start
  7.3 0.7 all-gather.6.cloned.1.call-update
  8.0 0.0 all-reduce.4.cloned.1.call-start
  8.1 33.1 %all-gather = s32[16,1,32]{2,1,0:T(1,128)S(1)} all-gather(s32[1,1,32]{2,1,0:T(1,128)} %bitcast.47), channel_id=1, replica_groups=mesh['row'=8,'col'=8,'depth'=2] {'col','depth'}, dimensions={0}, use_global_device_ids=true | all-gather | bytes 2176 | tf_op jit(solution)/shard_map/all_gather | solution.py:50
  41.2 0.1 copy.20
  41.3 0.1 reshape.50
  41.4 1.2 dynamic-slice
  43.3 0.1 broadcast_select_fusion
  43.4 0.8 bitcast_dynamic-update-slice_fusion
  44.1 17.3 %all-reduce.1 = (s32[256]{0:T(256)S(1)}, s32[16,16]{0,1:T(8,128)S(1)}) all-reduce(s32[256]{0:T(256)S(1)} %bitcast_dynamic-update-slice_fusion, s32[16,16]{0,1:T(8,128)S(1)} %bitcast.44), channel_id=1, replica_groups=mesh['row'=8,'col'=8,'depth'=2] {'row'}, use_global_device_ids=true, to_apply=%add | all-reduce | flops 512 | bytes 4096
  61.4 0.1 copy.23
  61.5 0.1 fusion
  61.6 0.0 all-gather.4.cloned.1.call-done
  61.6 4.1 copy.19
  65.8 88.3 %all-gather.6.cloned.1.call-done = bf16[32,16,4096]{2,0,1:T(8,128)(2,1)} async-done(((bf16[32,1,4096]{2,0,1:T(8,128)(2,1)}), bf16[32,16,4096]{2,0,1:T(8,128)(2,1)}) %all-gather.6.cloned.1.call-update) | async-done | bytes 4194320 | tf_op jit(solution)/shard_map/all_gather | solution.py:49
  154.1 2.0 dynamic-slice_select_fusion
  156.1 5.6 reshape.46
  161.6 0.0 all-reduce.4.cloned.1.call-update
  161.7 0.0 reduce-scatter.2.cloned.1.call-start
  161.7 12.4 %broadcast_multiply_fusion = bf16[256,16,64,64]{0,3,1,2:T(8,128)(2,1)} fusion(bf16[256,64,64]{0,2,1:T(8,128)(2,1)} %bitcast.41, bf16[256,16]{0,1:T(8,128)(2,1)S(1)} %fusion.1), kind=kLoop, calls=%fused_computation.2 | loop fusion | flops 16777216 | bytes 35659776 | tf_op jit(solution)/shard_map/rgkyz,rgkc->rygcz/dot_general | solution.py:22
  174.2 46.2 %copy.21 = bf16[256,64,1024]{2,1,0:T(8,128)(2,1)} copy(bf16[256,64,1024]{0,2,1:T(8,128)(2,1)} %bitcast.39) | data formatting | bytes 67108864 | tf_op jit(solution)/shard_map/reshape;reshape | solution.py:31
  220.3 7.3 %gather_fusion = bf16[64,64,1024]{2,1,0:T(8,128)(2,1)} fusion(bf16[256,64,1024]{2,1,0:T(8,128)(2,1)} %copy.21, s32[1024]{0:T(1024)S(1)} %pad_clamp_fusion), kind=kCustom, calls=%fused_computation | custom fusion | bytes 16777472 | tf_op jit(solution)/shard_map/gather | solution.py:32
  227.6 1.5 slice.10
  229.1 0.3 copy.22
  229.4 1.1 reshape.45
  230.5 5.1 fusion.4
  235.6 0.6 all-reduce.4.cloned.1.call-done
  236.2 5.7 copy.24
  241.9 21.1 %multiply_bitcast_fusion = bf16[16,64,16,16,64]{4,3,2,1,0:T(8,128)(2,1)} fusion(bf16[16,16,64,64]{3,1,2,0:T(8,128)(2,1)S(1)} %copy.24, bf16[16,16,16]{2,1,0:T(8,128)(2,1)S(1)} %fusion), kind=kLoop, calls=%fused_computation.1 | loop fusion | flops 16777216 | bytes 35659776 | tf_op jit(solution)/shard_map/rgkyz,rgkc->rygcz/transpose | solution.py:22
  263.1 75.4 %reshape.47 = bf16[1024,16384]{1,0:T(8,128)(2,1)} reshape(bf16[16,64,16,16,64]{4,3,2,1,0:T(8,128)(2,1)} %multiply_bitcast_fusion) | data formatting | bytes 67108864 | tf_op jit(solution)/shard_map/reshape | solution.py:25
  338.4 18.3 %fusion.5 = f32[256,16384]{1,0:T(8,128)} fusion(bf16[256,1024]{1,0:T(8,128)(2,1)S(1)} %bitcast.42, bf16[1024,16384]{1,0:T(8,128)(2,1)} %reshape.47), kind=kOutput, calls=%fused_computation.24 | convolution fusion | flops 8589934592 | bytes 50855936 | tf_op jit(solution)/shard_map/dot_general | solution.py:61
  356.7 0.0 reduce-scatter.2.cloned.1.call-update
  356.7 355.4 %reduce-scatter.2.cloned.1.call-done = f32[256,1024]{1,0:T(8,128)} async-done(((f32[256,16384]{1,0:T(8,128)}), f32[256,1024]{1,0:T(8,128)}) %reduce-scatter.2.cloned.1.call-update) | async-done | bytes 1048592 | tf_op jit(solution)/shard_map/reduce_scatter | solution.py:62
  712.1 2.4 bitcast_subtract_fusion
  (6 shorter events, 0.0 us)
Async XLA Ops:
  6.5 55.1 %all-gather.4.cloned.1.call-start = ((), (), s32[]{:S(2)}) async-start(), calls=%async_computation.1 | async-start | bytes 2359296 | tf_op jit(solution)/shard_map/all_gather | solution.py:44
  7.3 146.8 %all-gather.6.cloned.1.call-start = ((), (), s32[]{:S(2)}) async-start(), calls=%async_computation.2 | async-start | bytes 4456448 | tf_op jit(solution)/shard_map/all_gather | solution.py:49
  8.0 228.2 %all-reduce.4.cloned.1.call-start = ((), (), s32[]{:S(2)}) async-start(), calls=%async_computation.3 | async-start | bytes 8388608 | tf_op jit(solution)/shard_map/psum | solution.py:13
  161.7 550.5 %reduce-scatter.2.cloned.1.call-start = ((), (), s32[]{:S(2)}) async-start(), calls=%async_computation.4 | async-start | bytes 17825792 | tf_op jit(solution)/shard_map/reduce_scatter | solution.py:62
Sparse Core Ops, SparseCore 0:
  9.1 28.9 all-gather.3
  39.8 114.2 all-gather.5
  161.8 74.3 all-reduce.3
  356.9 355.2 reduce-scatter.1
where the time goes:
time: 725 us; the launch traced here: 721 us
  waiting for transfers between devices  446 us (62%)
  local copies, waits for them, and re-layouts  149 us (21%)
  blocking collectives  50.4 us (7%)
  other arithmetic  38.2 us (5%)
  matrix products  23.4 us (3%)
  between operations  13.9 us (2%)
    reduce_scatter x1, waiting for transfers between devices, body(): lax.psum_scatter(partial_value, ('col', 'depth'), scatter_dimension=1, ti...  355 us
    all_gather x1, waiting for transfers between devices, body(): lax.all_gather(blocks, ('col', 'depth'), axis=1, tiled=True)  88.3 us
    reshape x1, local copies, waits for them, and re-layouts, densify(): return dense_tiles.reshape(rows * BLOCK, groups * group_width * BLOCK)  75.4 us
    another operation x1, local copies, waits for them, and re-layouts, slab_square(): panel_blocks = panel_dense.reshape(-1, BLOCK, width)  46.2 us
    all_gather x1, blocking collectives, body(): lax.all_gather(pattern, ('col', 'depth'), axis=1, tiled=True)  33.1 us
    transpose x1, other arithmetic, densify(): jnp.einsum('rgkyz,rgkc->rygcz', tile_grid, onehot, preferred_element_type...  21.1 us
    dot_general x1, matrix products, body(): jnp.dot(square, group_dense, preferred_element_type=jnp.float32)  18.3 us
    unnamed x1, blocking collectives  17.3 us
  transfers between devices with their start and end apart: 4, of which 3 were waited for; matrix products, arithmetic and copies ran while one was open for 11% of the time, Pallas kernels for 0%

commit v1 on v0

--- a/solution.py
+++ b/solution.py
@@ -46,7 +46,12 @@
     )
     panel_dense = densify(column_tiles, column_ids, group_width)
     row_tiles, row_ids = (
-        lax.all_gather(blocks, ("col", "depth"), axis=1, tiled=True),
+        jnp.concatenate(
+            lax.all_to_all(
+                jnp.stack([blocks] * lax.axis_size(("col", "depth"))), ("col", "depth"), 0, 0
+            ),
+            axis=1,
+        ),
         lax.all_gather(pattern, ("col", "depth"), axis=1, tiled=True),
     )
     square32 = slab_square(row_tiles[:SR], row_ids[:SR], panel_dense)

time: 725 us -> 696 us (0.960)
  waiting for transfers between devices: 446 us -> 350 us
  blocking collectives: 50.4 us -> 107 us
  starting transfers between devices: 0.12 us -> 7.94 us
    all_gather x1 -> x0, waiting for transfers between devices: 88.3 us -> none  [body(): lax.all_gather(blocks, ('col', 'depth'), axis=1, tiled=True)]
    all_gather x1, blocking collectives: 33.1 us -> 90.2 us  [body(): lax.all_gather(pattern, ('col', 'depth'), axis=1, tiled=True)]
    all_to_all x0 -> x1, starting transfers between devices: none -> 7.64 us  [body(): lax.all_to_all(jnp.stack([blocks] * lax.axis_size(('col', 'depth'))), ('c...]
  transfers between devices with their start and end apart: 4 -> 4, of which waited for: 3 -> 1; matrix products, arithmetic and copies ran while one was open for 11% -> 11% of each run, Pallas kernels for 0% -> 0%
where the time goes in v1:
time: 696 us; the launch traced here: 692 us
  waiting for transfers between devices  350 us (50%)
  local copies, waits for them, and re-layouts  152 us (22%)
  blocking collectives  107 us (15%)
  other arithmetic  38.5 us (6%)
  matrix products  23.3 us (3%)
  between operations  13.9 us (2%)
  starting transfers between devices  7.94 us (1%)
    reduce_scatter x1, waiting for transfers between devices, body(): lax.psum_scatter(partial_value, ('col', 'depth'), scatter_dimension=1, ti...  350 us
    all_gather x1, blocking collectives, body(): lax.all_gather(pattern, ('col', 'depth'), axis=1, tiled=True)  90.2 us
    reshape x1, local copies, waits for them, and re-layouts, densify(): return dense_tiles.reshape(rows * BLOCK, groups * group_width * BLOCK)  75.4 us
    another operation x1, local copies, waits for them, and re-layouts, slab_square(): panel_blocks = panel_dense.reshape(-1, BLOCK, width)  46.2 us
    transpose x1, other arithmetic, densify(): jnp.einsum('rgkyz,rgkc->rygcz', tile_grid, onehot, preferred_element_type...  21.2 us
    dot_general x1, matrix products, body(): jnp.dot(square, group_dense, preferred_element_type=jnp.float32)  18.3 us
    unnamed x1, blocking collectives  16.5 us
  transfers between devices with their start and end apart: 4, of which 1 were waited for; matrix products, arithmetic and copies ran while one was open for 11% of the time, Pallas kernels for 0%

profile of v1, /device:TPU:1, one launch (start us, length us, event | category | flops | bytes accessed | tf_op | source)
XLA Modules:
  0.0 692.4 jit_solution(12669175086182912)
XLA Ops:
  6.5 0.0 copy-start.1
  6.5 0.0 copy-start
  6.5 3.4 stack.2
  10.0 7.6 %all-to-all-start = ((bf16[16,32,1,4096]{3,1,2,0:T(8,128)(2,1)}), bf16[16,32,1,4096]{3,1,2,0:T(8,128)(2,1)}, u32[]{:S(2)}, u32[]{:S(2)}) async-start(bf16[16,32,1,4096]{3,1,2,0:T(8,128)(2,1)} %stack.2), calls=%async_computation | async-start | bytes 8388608 | tf_op jit(solution)/shard_map/all_to_all | solution.py:50
  17.6 0.0 all-gather.3.cloned.1.call-start
  17.7 0.7 all-gather.3.cloned.1.call-update
  18.3 0.0 all-reduce.4.cloned.1.call-start
  18.4 0.0 copy-done
  18.4 90.2 %all-gather = s32[16,1,32]{2,1,0:T(1,128)S(1)} all-gather(s32[1,1,32]{2,1,0:T(1,128)S(1)} %bitcast.58), channel_id=1, replica_groups=mesh['row'=8,'col'=8,'depth'=2] {'col','depth'}, dimensions={0}, use_global_device_ids=true | all-gather | bytes 2176 | tf_op jit(solution)/shard_map/all_gather | solution.py:55
  108.6 0.1 copy.16
  108.7 0.1 reshape.65
  108.8 0.0 copy-done.1
  108.8 0.6 dynamic-slice.2
  110.0 0.1 broadcast_select_fusion
  110.1 0.1 bitcast_dynamic-update-slice_fusion
  110.2 16.5 %all-reduce.1 = (s32[256]{0:T(256)S(1)}, s32[16,16]{0,1:T(8,128)S(1)}) all-reduce(s32[256]{0:T(256)S(1)} %bitcast_dynamic-update-slice_fusion, s32[16,16]{0,1:T(8,128)S(1)} %bitcast.55), channel_id=1, replica_groups=mesh['row'=8,'col'=8,'depth'=2] {'row'}, use_global_device_ids=true, to_apply=%add | all-reduce | flops 512 | bytes 4096
  126.7 0.1 copy.19
  126.8 0.1 fusion
  126.9 0.0 all-gather.3.cloned.1.call-done
  127.0 4.1 copy.15
  131.1 0.0 all-to-all-done
  131.1 2.0 select_bitcast_fusion
  133.1 5.6 reshape.60
  138.7 0.0 all-reduce.4.cloned.1.call-update
  138.7 0.2 reduce-scatter.2.cloned.1.call-start
  138.9 12.7 %broadcast_multiply_fusion = bf16[256,16,64,64]{0,3,1,2:T(8,128)(2,1)} fusion(bf16[256,64,64]{0,2,1:T(8,128)(2,1)} %bitcast.51, bf16[256,16]{0,1:T(8,128)(2,1)S(1)} %fusion.1), kind=kLoop, calls=%fused_computation.2 | loop fusion | flops 16777216 | bytes 35659776 | tf_op jit(solution)/shard_map/rgkyz,rgkc->rygcz/dot_general | solution.py:22
  151.6 46.2 %copy.17 = bf16[256,64,1024]{2,1,0:T(8,128)(2,1)} copy(bf16[256,64,1024]{0,2,1:T(8,128)(2,1)} %bitcast.49) | data formatting | bytes 67108864 | tf_op jit(solution)/shard_map/reshape;reshape | solution.py:31
  197.8 7.5 %gather_fusion = bf16[64,64,1024]{2,1,0:T(8,128)(2,1)} fusion(bf16[256,64,1024]{2,1,0:T(8,128)(2,1)} %copy.17, s32[1024]{0:T(1024)S(1)} %pad_clamp_fusion), kind=kCustom, calls=%fused_computation | custom fusion | bytes 16777472 | tf_op jit(solution)/shard_map/gather | solution.py:32
  205.2 1.4 slice.11
  206.7 0.3 copy.18
  207.0 1.1 reshape.59
  208.1 5.0 fusion.4
  213.1 0.0 all-reduce.4.cloned.1.call-done
  213.2 5.7 copy.20
  218.9 21.2 %multiply_bitcast_fusion = bf16[16,64,16,16,64]{4,3,2,1,0:T(8,128)(2,1)} fusion(bf16[16,16,64,64]{3,1,2,0:T(8,128)(2,1)S(1)} %copy.20, bf16[16,16,16]{2,1,0:T(8,128)(2,1)S(1)} %fusion), kind=kLoop, calls=%fused_computation.1 | loop fusion | flops 16777216 | bytes 35659776 | tf_op jit(solution)/shard_map/rgkyz,rgkc->rygcz/transpose | solution.py:22
  240.1 75.4 %reshape.61 = bf16[1024,16384]{1,0:T(8,128)(2,1)} reshape(bf16[16,64,16,16,64]{4,3,2,1,0:T(8,128)(2,1)} %multiply_bitcast_fusion) | data formatting | bytes 67108864 | tf_op jit(solution)/shard_map/reshape | solution.py:25
  315.5 18.3 %fusion.5 = f32[256,16384]{1,0:T(8,128)} fusion(bf16[256,1024]{1,0:T(8,128)(2,1)S(1)} %bitcast.52, bf16[1024,16384]{1,0:T(8,128)(2,1)} %reshape.61), kind=kOutput, calls=%fused_computation.24 | convolution fusion | flops 8589934592 | bytes 50855936 | tf_op jit(solution)/shard_map/dot_general | solution.py:66
  333.8 0.0 reduce-scatter.2.cloned.1.call-update
  333.8 349.6 %reduce-scatter.2.cloned.1.call-done = f32[256,1024]{1,0:T(8,128)} async-done(((f32[256,16384]{1,0:T(8,128)}), f32[256,1024]{1,0:T(8,128)}) %reduce-scatter.2.cloned.1.call-update) | async-done | bytes 1048592 | tf_op jit(solution)/shard_map/reduce_scatter | solution.py:67
  683.5 2.4 bitcast_subtract_fusion
  (6 shorter events, 0.0 us)
Async XLA Ops:
  6.5 102.3 %copy-start.1 = (u32[128]{0:T(128)S(1)}, u32[128]{0:T(128)}, u32[]{:S(2)}) copy-start(u32[128]{0:T(128)} %constant.78) | copy-start | bytes 1540
  6.5 11.9 %copy-start = (s32[32,1]{0,1:T(1,128)S(1)}, s32[32,1]{0,1:T(1,128)}, u32[]{:S(2)}) copy-start(s32[32,1]{0,1:T(1,128)} %param.3) | copy-start | bytes 388
  10.0 121.1 %all-to-all-start = ((bf16[16,32,1,4096]{3,1,2,0:T(8,128)(2,1)}), bf16[16,32,1,4096]{3,1,2,0:T(8,128)(2,1)}, u32[]{:S(2)}, u32[]{:S(2)}) async-start(bf16[16,32,1,4096]{3,1,2,0:T(8,128)(2,1)} %stack.2), calls=%async_computation | async-start | bytes 8388608 | tf_op jit(solution)/shard_map/all_to_all | solution.py:50
  17.6 109.4 %all-gather.3.cloned.1.call-start = ((), (), s32[]{:S(2)}) async-start(), calls=%async_computation.2 | async-start | bytes 2359296 | tf_op jit(solution)/shard_map/all_gather | solution.py:44
  18.3 194.8 %all-reduce.4.cloned.1.call-start = ((), (), s32[]{:S(2)}) async-start(), calls=%async_computation.3 | async-start | bytes 8388608 | tf_op jit(solution)/shard_map/psum | solution.py:13
  138.7 544.7 %reduce-scatter.2.cloned.1.call-start = ((), (), s32[]{:S(2)}) async-start(), calls=%async_computation.4 | async-start | bytes 17825792 | tf_op jit(solution)/shard_map/reduce_scatter | solution.py:67
Sparse Core Ops, SparseCore 0:
  20.2 28.5 all-gather.2
  138.8 68.5 all-reduce.3
  333.9 349.4 reduce-scatter.1
